TPU v7x, 256 devices: a whole 4x4x8 slice. The times are simulated.
256 devices in a mesh: row: 8 (over x_lo, y), col: 32 (over x_hi, z, core).
Axes of the slice: x: 4 (x_hi: 2, x_lo: 2; x = x_hi * 2 + x_lo), y: 4, z: 8, core: 2. Of those that a mesh axis runs over, the one named last changes fastest.
Arguments:
- sigma_sep: float32 [4096, 4096], P('col', 'row')
- factor_one: float32 [16384, 4096], P('col', 'row'), may hold values from -0.109375 to 0.109375
- inverse_one: float32 [128, 128, 128], P('col')
- list_one: int32 [128, 24], P('col'), may hold values from -1 to 31, as said below
- factor_two: float32 [16384, 4096], P('col', 'row'), may hold values from -0.109375 to 0.109375
- factor_link: float32 [128, 128, 128], P('col'), may hold values from -0.5 to 0.5
- inverse_two: float32 [128, 128, 128], P('col')
- list_two: int32 [128, 24], P('col'), may hold values from -1 to 31, as said below
Outputs:
- cross_one: float32 [16384, 4096], P('col', 'row')
- diag_one: float32 [128, 128, 128], P('col')
- cross_two: float32 [16384, 4096], P('col', 'row')
- link_two: float32 [128, 128, 128], P('col')
- diag_two: float32 [128, 128, 128], P('col')
Inputs may be any that keep to these rules, and one draw needn't show every extreme that they name: Each row of list_one names distinct separator tiles followed by -1 entries; some row names 24 tiles and some row fewer. Row s of list_two keeps some of the tiles of row s of list_one at their places and holds -1 elsewhere.
All inputs are finite; a program needn't handle non-finite values.
Results may differ from a plain program's by a relative error of at most 0.000076.
Values sent between devices are 32-bit elements; how exact they have to be, the bound alone decides.
A program may use at most 192 MiB of HBM per device.

v0:
```python
import jax
import jax.numpy as jnp
from jax import lax
from jax.sharding import PartitionSpec as P

TILE = 128


highest = lax.Precision.HIGHEST


def tile_hits(lists, row_len):
    tile_count = row_len // TILE
    tile_ids = lax.axis_index("row") * tile_count + jnp.arange(tile_count, dtype=jnp.int32)
    marks = jnp.sum((lists[:, :, None] == tile_ids[None, None, :]).astype(jnp.float32), axis=1)
    return jnp.repeat(marks, TILE, axis=1)[:, None, :]


def local(
    sigma_sep, factor_one, inverse_one, list_one, factor_two, factor_link, inverse_two, list_two
):
    local_count = inverse_one.shape[0]
    row_len = factor_one.shape[1]
    block_rows = local_count * TILE
    hits_one = tile_hits(list_one, row_len)
    hits_two = tile_hits(list_two, row_len)
    lower_one = factor_one.reshape(local_count, TILE, row_len) * hits_one
    upper_one = jnp.einsum("sij,sia->sja", inverse_one, lower_one, precision=highest)
    lower_two = factor_two.reshape(local_count, TILE, row_len) * hits_two
    upper_two = jnp.einsum("sij,sia->sja", inverse_two, lower_two, precision=highest)
    link_upper = jnp.einsum("sij,spi->sjp", inverse_two, factor_link, precision=highest)
    stacked = jnp.concatenate(
        [upper_one.reshape(block_rows, row_len), upper_two.reshape(block_rows, row_len)], axis=0
    )
    gathered = lax.all_gather(stacked, "row", axis=1, tiled=True)
    products = jnp.dot(
        gathered,
        lax.all_gather(sigma_sep, "col", axis=0, tiled=True),
        precision=highest,
        preferred_element_type=jnp.float32,
    )
    prod_one = products[:block_rows].reshape(local_count, TILE, row_len)
    prod_two = products[block_rows:].reshape(local_count, TILE, row_len)
    cross_one = -(hits_one * prod_one)
    prod_two = prod_two + jnp.einsum("sjp,spa->sja", link_upper, cross_one, precision=highest)
    cross_two = -(hits_two * prod_two)
    part_one = jnp.einsum("sja,ska->sjk", upper_one, prod_one, precision=highest)
    part_link = jnp.einsum("spa,ska->spk", cross_one, upper_two, precision=highest)
    part_two = jnp.einsum("sja,ska->sjk", upper_two, prod_two, precision=highest)
    gram_one = jnp.einsum("sij,sik->sjk", inverse_one, inverse_one, precision=highest)
    gram_two = jnp.einsum("sij,sik->sjk", inverse_two, inverse_two, precision=highest)
    diag_one = gram_one + lax.psum(part_one, "row")
    members = (part_link, part_two)
    summed = lax.psum((members[0], members[1]), "row")
    link_prod = summed[0] + jnp.einsum("spq,skq->spk", diag_one, link_upper, precision=highest)
    diag_two = (
        gram_two + summed[1] + jnp.einsum("sjp,spk->sjk", link_upper, link_prod, precision=highest)
    )
    return (
        cross_one.reshape(block_rows, row_len),
        diag_one,
        cross_two.reshape(block_rows, row_len),
        -link_prod,
        diag_two,
    )


def solution(mesh):
    placed = (
        P("col", "row"),
        P("col", "row"),
        P("col", None, None),
        P("col", None),
        P("col", "row"),
        P("col", None, None),
        P("col", None, None),
        P("col", None),
    )
    return jax.shard_map(
        local,
        mesh=mesh,
        in_specs=placed,
        out_specs=(
            P("col", "row"),
            P("col", None, None),
            P("col", "row"),
            P("col", None, None),
            P("col", None, None),
        ),
        check_vma=False,
    )
```

profile of v0, /device:TPU:4, one launch (start us, length us, event | category | flops | bytes accessed | tf_op | source)
XLA Modules:
  0.0 418.5 jit_solution(10063386471048087188)
XLA Ops:
  7.2 0.0 copy-start
  7.2 0.0 copy-start.3
  7.2 0.0 all-gather.5.cloned.1.call-start
  7.2 0.7 all-gather.5.cloned.1.call-update
  7.9 0.0 all-gather.3.cloned.1.call-start
  8.0 0.9 convert_reduce_fusion
  8.8 0.1 broadcast_bitcast_fusion.1
  8.9 0.1 broadcast_bitcast_fusion
  9.0 2.4 fusion.3
  11.4 0.0 copy-done
  11.4 2.3 fusion.1
  13.7 1.5 pad_maximum_fusion
  15.2 0.0 all-gather.3.cloned.1.call-update
  15.3 0.0 all-reduce.3.cloned.1.call-start
  15.3 0.0 copy-done.3
  15.3 0.6 fusion.14
  15.9 96.8 %all-gather.5.cloned.1.call-done = f32[4096,512]{1,0:T(8,128)} async-done(((f32[128,512]{1,0:T(8,128)}), f32[4096,512]{1,0:T(8,128)}) %all-gather.5.cloned.1.call-update) | async-done | bytes 8388624 | tf_op jit(solution)/shard_map/all_gather | solution.py:38
  112.8 173.6 %all-gather.3.cloned.1.call-done = f32[1024,4096]{1,0:T(8,128)} async-done(((f32[1024,512]{1,0:T(8,128)}), f32[1024,4096]{1,0:T(8,128)}) %all-gather.3.cloned.1.call-update) | async-done | bytes 16777232 | tf_op jit(solution)/shard_map/all_gather | solution.py:35
  286.3 29.9 %fusion.12 = f32[1024,512]{1,0:T(8,128)S(1)} fusion(f32[1024,4096]{1,0:T(8,128)} %all-gather.3.cloned.1.call-done, f32[4096,512]{1,0:T(8,128)} %all-gather.5.cloned.1.call-done), kind=kOutput, calls=%fused_computation.28 | convolution fusion | flops 25769803776 | bytes 27262976 | tf_op jit(solution)/shard_map/dot_general | solution.py:36
  316.2 0.0 copy-start.1
  316.2 1.2 fusion.10
  317.5 1.9 fusion.5
  319.4 1.8 fusion.13
  321.2 2.1 multiply_negate_fusion
  323.3 1.8 fusion.15
  325.1 0.0 all-reduce.3.cloned.1.call-update
  325.1 80.2 %all-reduce.3.cloned.1.call-done = (f32[4,128,128]{2,1,0:T(8,128)}, f32[4,128,128]{2,1,0:T(8,128)}, f32[4,128,128]{2,1,0:T(8,128)}) async-done(((f32[4,128,128]{2,1,0:T(8,128)}, f32[4,128,128]{2,1,0:T(8,128)}, f32[4,128,128]{2,1,0:T(8,128)}), (f32[4,128,128]{2,1,0:T(8,128)}, f32[4,128,128]{2,1,0:T(8,128)}, f32[4,128,128]{2,1,0:T(8,128)})) %all-reduce.3.cloned.1.call-update) | async-done | bytes 786448 | tf_op jit(solution)/shard_map/psum | solution.py:52
  405.3 0.0 copy-done.1
  405.3 1.5 convolution_add_fusion.4
  406.8 0.0 copy-start.2
  406.9 1.6 convolution_add_fusion.2
  408.5 2.3 fusion.11
  410.8 1.1 convolution_add_fusion.1
  411.9 0.0 copy-done.2
  (3 shorter events, 0.0 us)
Async XLA Ops:
  7.2 4.2 %copy-start = (f32[4,128,128]{2,1,0:T(8,128)S(1)}, f32[4,128,128]{2,1,0:T(8,128)}, u32[]{:S(2)}) copy-start(f32[4,128,128]{2,1,0:T(8,128)} %param.14) | copy-start | bytes 786436
  7.2 8.1 %copy-start.3 = (f32[4,128,128]{2,1,0:T(8,128)S(1)}, f32[4,128,128]{2,1,0:T(8,128)}, u32[]{:S(2)}) copy-start(f32[4,128,128]{2,1,0:T(8,128)} %param.13) | copy-start | bytes 786436
  7.2 105.6 %all-gather.5.cloned.1.call-start = ((), (), s32[]{:S(2)}) async-start(), calls=%async_computation.1 | async-start | bytes 8650752 | tf_op jit(solution)/shard_map/all_gather | solution.py:38
  7.9 278.4 %all-gather.3.cloned.1.call-start = ((), (), s32[]{:S(2)}) async-start(), calls=%async_computation | async-start | bytes 18874368 | tf_op jit(solution)/shard_map/all_gather | solution.py:35
  15.3 390.0 %all-reduce.3.cloned.1.call-start = ((), (), s32[]{:S(2)}) async-start(), calls=%async_computation.2 | async-start | bytes 1572864 | tf_op jit(solution)/shard_map/psum | solution.py:52
  316.2 89.1 %copy-start.1 = (f32[4,128,128]{2,1,0:T(8,128)S(1)}, f32[4,128,128]{2,1,0:T(8,128)}, u32[]{:S(2)}) copy-start(f32[4,128,128]{2,1,0:T(8,128)} %param.10) | copy-start | bytes 786436
  406.8 5.1 %copy-start.2 = (f32[4,128,128]{2,1,0:T(8,128)}, f32[4,128,128]{2,1,0:T(8,128)S(1)}, u32[]{:S(2)}) copy-start(f32[4,128,128]{2,1,0:T(8,128)S(1)} %convolution_add_fusion.4) | copy-start | bytes 786436
Sparse Core Ops, SparseCore 0:
  10.8 101.9 all-gather.4
  114.6 171.7 all-gather.2
  325.2 79.9 all-reduce.2
where the time goes:
time: 419 us; the launch traced here: 418 us
  waiting for transfers between devices  351 us (84%)
  matrix products  49.4 us (12%)
  between operations  13.9 us (3%)
    all_gather x1, waiting for transfers between devices, local(): gathered = lax.all_gather(stacked, 'row', axis=1, tiled=True)  174 us
    all_gather x1, waiting for transfers between devices, local(): lax.all_gather(sigma_sep, 'col', axis=0, tiled=True)  96.8 us
    psum x1, waiting for transfers between devices, local(): diag_one = gram_one + lax.psum(part_one, 'row')  80.2 us
    dot_general x1, matrix products, local(): jnp.dot(gathered, lax.all_gather(sigma_sep, 'col', axis=0, tiled=True), p...  29.9 us
  transfers between devices with their start and end apart: 3, of which 3 were waited for; matrix products, arithmetic and copies ran while one was open for 2% of the time, Pallas kernels for 0%

commit v1 on v0

v1 whole, which is shorter than its diff:
```python
import functools

import jax
import jax.numpy as jnp
from jax import lax
from jax.experimental import pallas as pl
from jax.experimental.pallas import tpu as pltpu
from jax.sharding import PartitionSpec as P

TILE = 128
MESH = pl.DeviceIdType.MESH
F32 = jnp.float32
BF16 = jnp.bfloat16
WIDE = 512
SUPERS = 4
CHUNKS = 8


def split(x):
    high = x.astype(BF16)
    low = (x - high.astype(F32)).astype(BF16)
    return high, low


def dot3(a, b, ca, cb):
    ah, al = split(a)
    bh, bl = split(b)
    dg = lambda u, v: lax.dot_general(u, v, (((ca,), (cb,)), ((), ())), preferred_element_type=F32)
    return dg(ah, bh) + (dg(ah, bl) + dg(al, bh))


def kernel(
    sig, f1, i1, n1, f2, fl, i2, n2,
    c1, d1, c2, l2, d2,
    H, A, As, B, Bh, Bl, Cs, Cr, Po, P1, R1, G1, P2, R2, G2, LU,
    as_s, as_r, af_s, af_r, bx_s, bx_r, bz_s, bz_r, bc_s, bc_r, c_s, c_r, r1_s, r1_r, g1_s, g1_r, r2_s, r2_r, g2_s, g2_r,
):
    row = lax.axis_index("row")
    col = lax.axis_index("col")
    xl, y = row // 4, row % 4
    xh, z, c = col // 16, (col // 2) % 8, col % 2
    sends = []

    def remote(src, dst, ss, rs, dev):
        return pltpu.make_async_remote_copy(
            src_ref=src, dst_ref=dst, send_sem=ss, recv_sem=rs, device_id=dev, device_id_type=MESH
        )

    def start(*args):
        copy = remote(*args)
        copy.start()
        sends.append(copy)

    def arrived(ref, sem):
        pltpu.make_async_copy(ref, ref, sem).wait()

    right, left = (xl * 4 + (y + 1) % 4, col), (xl * 4 + (y + 3) % 4, col)
    pair = ((1 - xl) * 4 + y, col)
    up, down = (row, xh * 16 + ((z + 1) % 8) * 2 + c), (row, xh * 16 + ((z + 7) % 8) * 2 + c)
    twin = (row, xh * 16 + z * 2 + (1 - c))
    other_col = (1 - xh) * 16 + z * 2 + c
    peers = [((row + i) % 8, col) for i in range(1, 8)]
    barrier = pltpu.get_barrier_semaphore()
    for dev in peers + [up, down, twin, (row, other_col), ((1 - xl) * 4 + y, other_col)]:
        pl.semaphore_signal(barrier, inc=1, device_id=dev, device_id_type=MESH)

    for level, lists in enumerate((n1, n2)):
        for t in range(4):
            match = jnp.where(lists[...] == row * 4 + t, 1.0, 0.0).astype(F32)
            mark = jnp.sum(match, axis=1, keepdims=True)
            H[level, :, t * TILE:(t + 1) * TILE] = jnp.broadcast_to(mark, (SUPERS, TILE))

    def hits(level, s):
        return H[level, s:s + 1, :]

    def upper(q):
        level, s = q // SUPERS, q % SUPERS
        f, inv = ((f1, i1), (f2, i2))[level]
        masked = f[s * TILE:(s + 1) * TILE, :] * hits(level, s)
        A[y, q * TILE:(q + 1) * TILE, :] = dot3(inv[s].T, masked, 1, 0)

    def a_block(slot, first, count):
        return A.at[slot, pl.ds(first, count), :]

    def a_send(q):
        for d, dev in enumerate((right, left)):
            ref = a_block(y, q * TILE, TILE)
            start(ref, ref, as_s.at[d, q], as_r.at[d, q], dev)

    def a_forward(q):
        for d, dev in enumerate((right, left)):
            slot = (y + (3, 1)[d]) % 4
            arrived(a_block(slot, q * TILE, TILE), as_r.at[d, q])
            ref = a_block(slot, q * TILE + d * 64, 64)
            start(ref, ref, af_s.at[d, q], af_r.at[d, q], dev)

    def a_ready(q):
        for d in range(2):
            arrived(a_block((y + 2) % 4, q * TILE + d * 64, 64), af_r.at[d, q])
        for k in range(4):
            high, low = split(A[k, q * TILE:(q + 1) * TILE, :])
            As[q, 0:TILE, k * WIDE:(k + 1) * WIDE] = high
            As[q, TILE:2 * TILE, k * WIDE:(k + 1) * WIDE] = low

    def b_rows(k, zs, core, h):
        first = pl.multiple_of(((zs + 8) % 8 * 2 + core) * TILE + h * 64, 64)
        return B.at[(1 - xl, xl)[k], pl.ds(first, 64), :]

    def b_spread(k):
        for h in range(2):
            src = sig.at[pl.ds(h * 64, 64), :]
            dst = B.at[xl, pl.ds(pl.multiple_of((z * 2 + c) * TILE + h * 64, 64), 64), :]

            def out(i, colt):
                return remote(src, dst, bx_s.at[i, h], bx_r.at[k, h], (xh * 4 + y, colt))

            if k == 0:
                @pl.when(xl != xh)
                def _():
                    out(0, z * 2 + c).start()
                    out(1, 16 + z * 2 + c).start()
            else:
                @pl.when(xl == xh)
                def _():
                    pltpu.make_async_copy(src, dst, bx_r.at[k, h]).start()
                    out(0, other_col).start()

    def b_spread_done():
        for h in range(2):
            src = sig.at[pl.ds(h * 64, 64), :]
            remote(src, src, bx_s.at[0, h], bx_r.at[0, h], pair).wait_send()

            @pl.when(xl != xh)
            def _():
                remote(src, src, bx_s.at[1, h], bx_r.at[0, h], pair).wait_send()

    def b_pass(k, d, s, h):
        ref = b_rows(k, z + (-s, s)[d], c, h)
        start(ref, ref, bz_s.at[k, d, s, h], bz_r.at[k, d, s, h], (up, down)[d])

    def b_twin(k, d, s, h):
        ref = b_rows(k, z + (-s, s)[d], c, h)
        start(ref, ref, bc_s.at[k, d, s, h], bc_r.at[k, d, s, h], twin)

    def b_home(k):
        for h in range(2):
            arrived(b_rows(k, z, c, h), bx_r.at[k, h])
            b_pass(k, 0, 0, h)
            b_pass(k, 1, 0, h)
            b_twin(k, 0, 0, h)

    def b_step(k, s, h):
        for d in range(2):
            arrived(b_rows(k, z + (-s, s)[d], c, h), bz_r.at[k, d, s - 1, h])
            if s < 3 or h == d:
                b_pass(k, d, s, h)
            b_twin(k, d, s, h)

    def b_last(k):
        for d in range(2):
            arrived(b_rows(k, z + 4, c, d), bz_r.at[k, d, 3, d])
            b_twin(k, d, 4, d)
        for h in range(2):
            arrived(b_rows(k, z, 1 - c, h), bc_r.at[k, 0, 0, h])
            for d in range(2):
                for s in range(1, 4):
                    arrived(b_rows(k, z + (-s, s)[d], 1 - c, h), bc_r.at[k, d, s, h])
            arrived(b_rows(k, z + 4, 1 - c, h), bc_r.at[k, h, 4, h])
        which = (1 - xl, xl)[k]

        def cut(i, carry):
            rows = pl.ds(pl.multiple_of(i * TILE, TILE), TILE)
            high, low = split(B[which, rows, :])
            Bh[which, rows, :] = high
            Bl[which, rows, :] = low
            return carry

        lax.fori_loop(0, 16, cut, 0)

    def product(q, k, out):
        which = (1 - xl, xl)[k]
        total = None
        for step in range(4):
            ks = slice(step * WIDE, (step + 1) * WIDE)
            both = jnp.dot(As[q, :, ks], Bh[which, ks, :], preferred_element_type=F32)
            rest = jnp.dot(As[q, 0:TILE, ks], Bl[which, ks, :], preferred_element_type=F32)
            term = both[0:TILE] + (both[TILE:2 * TILE] + rest)
            total = term if total is None else total + term
        out[q, :, :] = total

    def c_send(q):
        product(q, 0, Cs)
        start(Cs.at[q], Cr.at[q], c_s.at[q], c_r.at[q], pair)

    def own_upper(q):
        return A[y, q * TILE:(q + 1) * TILE, :]

    def finish_one(s):
        arrived(Cr.at[s], c_r.at[s])
        prod = Po[s] + Cr[s]
        cross = -(hits(0, s) * prod)
        c1[s * TILE:(s + 1) * TILE, :] = cross
        P1[:, s] = dot3(own_upper(s), prod, 1, 1).reshape(8, 16, TILE)
        P1[:, SUPERS + s] = dot3(cross, own_upper(SUPERS + s), 1, 1).reshape(8, 16, TILE)

    def finish_two(s):
        q = SUPERS + s
        arrived(Cr.at[q], c_r.at[q])
        prod = Po[q] + Cr[q] + dot3(LU[s], c1[s * TILE:(s + 1) * TILE, :], 1, 0)
        c2[s * TILE:(s + 1) * TILE, :] = -(hits(1, s) * prod)
        P2[:, s] = dot3(own_upper(q), prod, 1, 1).reshape(8, 16, TILE)

    def scatter(part, got, ss, rs):
        for i, dev in enumerate(peers):
            start(part.at[dev[0]], got.at[i], ss.at[i], rs.at[i], dev)

    def gather(part, got, whole, waits, ss, rs):
        total = part[row]
        for i in range(7):
            arrived(got.at[i], waits.at[i])
            total = total + got[i]
        whole[row] = total
        for i, dev in enumerate(peers):
            start(whole.at[row], whole.at[row], ss.at[i], rs.at[i], dev)

    def gathered(whole, waits):
        for i in range(7):
            arrived(whole.at[(row + 7 - i) % 8], waits.at[i])

    def side():
        for s in range(SUPERS):
            t1, t2 = i1[s].T, i2[s].T
            LU[s] = dot3(t2, fl[s], 1, 1)
            d1[s] = dot3(t1, t1, 1, 1)
            d2[s] = dot3(t2, t2, 1, 1)

    def tiles_one():
        gathered(G1, g1_r)
        for s in range(SUPERS):
            diag = d1[s] + G1[:, s].reshape(TILE, TILE)
            d1[s] = diag
            link = G1[:, SUPERS + s].reshape(TILE, TILE) + dot3(diag, LU[s], 1, 1)
            l2[s] = -link
            d2[s] = d2[s] + dot3(LU[s], link, 1, 0)

    upper(0)
    pl.semaphore_wait(barrier, 12)
    b_spread(0)
    a_send(0)
    upper(1)
    a_send(1)
    upper(2)
    a_send(2)
    upper(3)
    b_home(0)
    b_spread(1)
    upper(4)
    upper(5)
    a_forward(0)
    a_send(3)
    b_step(0, 1, 0)
    b_step(0, 1, 1)
    upper(6)
    upper(7)
    a_forward(1)
    a_send(4)
    b_step(0, 2, 0)
    b_step(0, 2, 1)
    side()
    b_step(0, 3, 0)
    a_forward(2)
    a_send(5)
    b_step(0, 3, 1)
    b_home(1)
    b_last(0)
    a_ready(0)
    c_send(0)
    a_forward(3)
    a_send(6)
    a_ready(1)
    b_step(1, 1, 0)
    c_send(1)
    b_step(1, 1, 1)
    a_ready(2)
    c_send(2)
    b_step(1, 2, 0)
    a_forward(4)
    a_send(7)
    b_step(1, 2, 1)
    a_ready(3)
    c_send(3)
    b_step(1, 3, 0)
    b_step(1, 3, 1)
    a_ready(4)
    c_send(4)
    a_forward(5)
    b_last(1)
    product(0, 1, Po)
    a_ready(5)
    c_send(5)
    finish_one(0)
    product(1, 1, Po)
    finish_one(1)
    a_forward(6)
    product(2, 1, Po)
    finish_one(2)
    a_ready(6)
    c_send(6)
    product(3, 1, Po)
    finish_one(3)
    scatter(P1, R1, r1_s, r1_r)
    a_forward(7)
    product(4, 1, Po)
    finish_two(0)
    product(5, 1, Po)
    finish_two(1)
    gather(P1, R1, G1, r1_r, g1_s, g1_r)
    a_ready(7)
    c_send(7)
    product(6, 1, Po)
    product(7, 1, Po)
    finish_two(2)
    tiles_one()
    finish_two(3)
    scatter(P2, R2, r2_s, r2_r)
    gather(P2, R2, G2, r2_r, g2_s, g2_r)
    gathered(G2, g2_r)
    for s in range(SUPERS):
        d2[s] = d2[s] + G2[:, s].reshape(TILE, TILE)
    b_spread_done()
    for copy in sends:
        copy.wait_send()


def local(
    sigma_sep, factor_one, inverse_one, list_one, factor_two, factor_link, inverse_two, list_two
):
    vmem = pl.BlockSpec(memory_space=pltpu.VMEM)
    wide = jax.ShapeDtypeStruct((SUPERS * TILE, WIDE), F32)
    tiles = jax.ShapeDtypeStruct((SUPERS, TILE, TILE), F32)
    dma = pltpu.SemaphoreType.DMA
    return pl.pallas_call(
        kernel,
        out_shape=(wide, tiles, wide, tiles, tiles),
        in_specs=[vmem] * 8,
        out_specs=(vmem,) * 5,
        scratch_shapes=[
            pltpu.VMEM((2, SUPERS, WIDE), F32),
            pltpu.VMEM((4, CHUNKS * TILE, WIDE), F32),
            pltpu.VMEM((CHUNKS, 2 * TILE, 4 * WIDE), BF16),
            pltpu.VMEM((2, 4 * WIDE, WIDE), F32),
            pltpu.VMEM((2, 4 * WIDE, WIDE), BF16),
            pltpu.VMEM((2, 4 * WIDE, WIDE), BF16),
            pltpu.VMEM((CHUNKS, TILE, WIDE), F32),
            pltpu.VMEM((CHUNKS, TILE, WIDE), F32),
            pltpu.VMEM((CHUNKS, TILE, WIDE), F32),
            pltpu.VMEM((8, 2 * SUPERS, 16, TILE), F32),
            pltpu.VMEM((7, 2 * SUPERS, 16, TILE), F32),
            pltpu.VMEM((8, 2 * SUPERS, 16, TILE), F32),
            pltpu.VMEM((8, SUPERS, 16, TILE), F32),
            pltpu.VMEM((7, SUPERS, 16, TILE), F32),
            pltpu.VMEM((8, SUPERS, 16, TILE), F32),
            pltpu.VMEM((SUPERS, TILE, TILE), F32),
            dma((2, CHUNKS)), dma((2, CHUNKS)), dma((2, CHUNKS)), dma((2, CHUNKS)),
            dma((2, 2)), dma((2, 2)),
            dma((2, 2, 4, 2)), dma((2, 2, 4, 2)),
            dma((2, 2, 5, 2)), dma((2, 2, 5, 2)),
            dma((CHUNKS,)), dma((CHUNKS,)),
            dma((7,)), dma((7,)), dma((7,)), dma((7,)),
            dma((7,)), dma((7,)), dma((7,)), dma((7,)),
        ],
        compiler_params=pltpu.CompilerParams(
            collective_id=0, has_side_effects=True, vmem_limit_bytes=60 * 2**20
        ),
        cost_estimate=pl.CostEstimate(
            flops=13_000_000_000, bytes_accessed=8_000_000, transcendentals=0
        ),
    )(sigma_sep, factor_one, inverse_one, list_one, factor_two, factor_link, inverse_two, list_two)


def solution(mesh):
    return jax.shard_map(
        local,
        mesh=mesh,
        in_specs=(
            P("col", "row"),
            P("col", "row"),
            P("col", None, None),
            P("col", None),
            P("col", "row"),
            P("col", None, None),
            P("col", None, None),
            P("col", None),
        ),
        out_specs=(
            P("col", "row"),
            P("col", None, None),
            P("col", "row"),
            P("col", None, None),
            P("col", None, None),
        ),
        check_vma=False,
    )
```

time: 419 us -> 127 us (0.30)
  waiting for transfers between devices: 351 us -> 0 us
  Pallas kernels: 0 us -> 120 us
  matrix products: 49.4 us -> 0 us
  between operations: 13.9 us -> 0.66 us
  local copies, waits for them, and re-layouts: 0.18 us -> 5.91 us
    all_gather x2 -> x0, waiting for transfers between devices: 270 us -> none  [the longest x1 174 us: local(): gathered = lax.all_gather(stacked, 'row', axis=1, tiled=True)]
    pallas_call x0 -> x1, Pallas kernels: none -> 120 us  [local(): pl.pallas_call(kernel, out_shape=(wide, tiles, wide, tiles, tiles), in_sp...]
    psum x1 -> x0, waiting for transfers between devices: 80.2 us -> none  [local(): diag_one = gram_one + lax.psum(part_one, 'row')]
    dot_general x12 -> x0, matrix products: 49.4 us -> none  [the longest x1 29.9 us: local(): jnp.dot(gathered, lax.all_gather(sigma_sep, 'col', axis=0, tiled=True), p...]
    unnamed x12 -> x13, local copies, waits for them, and re-layouts: 0.18 us -> 5.91 us
  transfers between devices with their start and end apart: 3 -> 0, of which waited for: 3 -> 0; matrix products, arithmetic and copies ran while one was open for 2% -> 0% of each run, Pallas kernels for 0% -> 0%
where the time goes in v1:
time: 127 us
  Pallas kernels  120 us (94%)
  local copies, waits for them, and re-layouts  5.91 us (5%)
    pallas_call x1, Pallas kernels, local(): pl.pallas_call(kernel, out_shape=(wide, tiles, wide, tiles, tiles), in_sp...  120 us
    unnamed x13, local copies, waits for them, and re-layouts  5.91 us

profile of v1, /device:TPU:4, one launch (start us, length us, event | category | flops | bytes accessed | tf_op | source)
XLA Modules:
  0.0 126.9 jit_solution(2787622984228874682)
XLA Ops:
  0.6 120.3 %shard_map.119 = (f32[512,512]{1,0:T(8,128)}, f32[4,128,128]{2,1,0:T(8,128)}, f32[512,512]{1,0:T(8,128)}, f32[4,128,128]{2,1,0:T(8,128)}, f32[4,128,128]{2,1,0:T(8,128)}) custom-call(f32[128,512]{1,0:T(8,128)} %sig.1, f32[512,512]{1,0:T(8,128)} %f1.1, f32[4,128,128]{2,1,0:T(8,128)} %i1.1, s32[4,24]{1,0:T(4,128)} %n1.1, f32[512,512]{1,0:T(8,128)} %f2.1, ...), custom_call_target="tpu_custom_call" | custom-call | flops 12999999488 | bytes 8000000 | tf_op jit(solution)/shard_map/pallas_call | solution.py:342
  120.9 0.0 copy-start.3
  120.9 0.0 copy-start
  121.0 2.4 %copy.18 = f32[512,512]{1,0:T(8,128)} copy(f32[512,512]{1,0:T(8,128)} %get-tuple-element.10) | data formatting | bytes 2097152
  123.3 0.0 copy-done.3
  123.3 0.7 copy.19
  124.0 0.0 copy-done
  124.0 0.0 copy-start.2
  124.0 1.0 copy.20
  125.0 0.1 copy-done.2
  125.1 0.0 copy-start.1
  125.1 0.7 copy.21
  125.8 0.3 copy-done.1
  126.2 0.7 copy.22
Async XLA Ops:
  120.9 2.4 %copy-start.3 = (f32[4,128,128]{2,1,0:T(8,128)S(1)}, f32[4,128,128]{2,1,0:T(8,128)}, u32[]{:S(2)}) copy-start(f32[4,128,128]{2,1,0:T(8,128)} %get-tuple-element.11) | copy-start | bytes 786436
  120.9 3.1 %copy-start = (f32[512,512]{1,0:T(8,128)S(1)}, f32[512,512]{1,0:T(8,128)}, u32[]{:S(2)}) copy-start(f32[512,512]{1,0:T(8,128)} %get-tuple-element.12) | copy-start | bytes 3145732
  124.0 1.1 copy-start.2
  125.1 1.0 copy-start.1

commit v2 on v1

--- a/solution.py
+++ b/solution.py
@@ -31,9 +31,10 @@
 
 def kernel(
     sig, f1, i1, n1, f2, fl, i2, n2,
-    c1, d1, c2, l2, d2,
-    H, A, As, B, Bh, Bl, Cs, Cr, Po, P1, R1, G1, P2, R2, G2, LU,
-    as_s, as_r, af_s, af_r, bx_s, bx_r, bz_s, bz_r, bc_s, bc_r, c_s, c_r, r1_s, r1_r, g1_s, g1_r, r2_s, r2_r, g2_s, g2_r,
+    o1, od1, o2, ol2, od2,
+    c1, d1, c2, l2, d2, F, Up, H, A, As, B, Bh, Bl, Cs, Cr, Po, P1, X1, Y1, G1, P2, R2, G2, P3, R3, G3, LU,
+    as_s, as_r, af_s, af_r, bx_s, bx_r, bz_s, bz_r, bc_s, bc_r, c_s, c_r, x1_s, x1_r, y1_s, y1_r, g1_s, g1_r, r2_s, r2_r, g2_s, g2_r,
+    r3_s, r3_r, g3_s, g3_r, f_r, u_s, u_r, o_s,
 ):
     row = lax.axis_index("row")
     col = lax.axis_index("col")
@@ -64,6 +65,13 @@
     for dev in peers + [up, down, twin, (row, other_col), ((1 - xl) * 4 + y, other_col)]:
         pl.semaphore_signal(barrier, inc=1, device_id=dev, device_id_type=MESH)
 
+    def load(q):
+        rows = pl.ds(q % SUPERS * TILE, TILE)
+        return pltpu.make_async_copy((f1, f2)[q // SUPERS].at[rows, :], F.at[q], f_r.at[q])
+
+    for q in range(CHUNKS):
+        load(q).start()
+
     for level, lists in enumerate((n1, n2)):
         for t in range(4):
             match = jnp.where(lists[...] == row * 4 + t, 1.0, 0.0).astype(F32)
@@ -75,8 +83,9 @@
 
     def upper(q):
         level, s = q // SUPERS, q % SUPERS
-        f, inv = ((f1, i1), (f2, i2))[level]
-        masked = f[s * TILE:(s + 1) * TILE, :] * hits(level, s)
+        inv = (i1, i2)[level]
+        load(q).wait()
+        masked = F[q, :, :] * hits(level, s)
         A[y, q * TILE:(q + 1) * TILE, :] = dot3(inv[s].T, masked, 1, 0)
 
     def a_block(slot, first, count):
@@ -200,15 +209,52 @@
         prod = Po[s] + Cr[s]
         cross = -(hits(0, s) * prod)
         c1[s * TILE:(s + 1) * TILE, :] = cross
-        P1[:, s] = dot3(own_upper(s), prod, 1, 1).reshape(8, 16, TILE)
-        P1[:, SUPERS + s] = dot3(cross, own_upper(SUPERS + s), 1, 1).reshape(8, 16, TILE)
-
-    def finish_two(s):
+        P1[0, s] = dot3(own_upper(s), prod, 1, 1)
+        P1[1, s] = dot3(cross, own_upper(SUPERS + s), 1, 1)
+
+    def linked(s):
+        q = SUPERS + s
+        Po[q] = Po[q] + dot3(LU[s], c1[s * TILE:(s + 1) * TILE, :], 1, 0)
+
+    def cross_two(s):
         q = SUPERS + s
         arrived(Cr.at[q], c_r.at[q])
-        prod = Po[q] + Cr[q] + dot3(LU[s], c1[s * TILE:(s + 1) * TILE, :], 1, 0)
+        prod = Po[q] + Cr[q]
         c2[s * TILE:(s + 1) * TILE, :] = -(hits(1, s) * prod)
-        P2[:, s] = dot3(own_upper(q), prod, 1, 1).reshape(8, 16, TILE)
+        return prod
+
+    def finish_two(s):
+        linked(s)
+        P2[:, s] = dot3(own_upper(SUPERS + s), cross_two(s), 1, 1).reshape(8, 16, TILE)
+
+    def send_upper(i):
+        start(A.at[y, pl.ds((6 + i) * TILE, TILE), :], Up.at[i], u_s.at[i], u_r.at[i], pair)
+
+    def last_two(i):
+        linked(2 + i)
+        arrived(Up.at[i], u_r.at[i])
+        part = dot3(own_upper(6 + i), Po[6 + i], 1, 1) + dot3(Up[i], Cs[6 + i], 1, 1)
+        P3[:, i] = part.reshape(8, 16, TILE)
+
+    def one_pair():
+        start(P1.at[1 - xl], X1, x1_s, x1_r, pair)
+
+    def one_ring():
+        arrived(X1, x1_r)
+        for s in range(SUPERS):
+            X1[s] = X1[s] + P1[xl, s]
+        for i in range(3):
+            to = (y + i + 1) % 4
+            start(X1.at[to], Y1.at[i], y1_s.at[i], y1_r.at[i], (xl * 4 + to, col))
+
+    def one_all():
+        total = X1[y]
+        for i in range(3):
+            arrived(Y1.at[i], y1_r.at[i])
+            total = total + Y1[i]
+        G1[xl, y] = total
+        for i, dev in enumerate(peers):
+            start(G1.at[xl, y], G1.at[xl, y], g1_s.at[i], g1_r.at[i], dev)
 
     def scatter(part, got, ss, rs):
         for i, dev in enumerate(peers):
@@ -235,18 +281,23 @@
             d2[s] = dot3(t2, t2, 1, 1)
 
     def tiles_one():
-        gathered(G1, g1_r)
+        for i in range(7):
+            sender = (row + 7 - i) % 8
+            arrived(G1.at[sender // 4, sender % 4], g1_r.at[i])
         for s in range(SUPERS):
-            diag = d1[s] + G1[:, s].reshape(TILE, TILE)
+            diag = d1[s] + G1[0, s]
             d1[s] = diag
-            link = G1[:, SUPERS + s].reshape(TILE, TILE) + dot3(diag, LU[s], 1, 1)
+            link = G1[1, s] + dot3(diag, LU[s], 1, 1)
             l2[s] = -link
             d2[s] = d2[s] + dot3(LU[s], link, 1, 0)
 
+    def write(i, src, dst):
+        return pltpu.make_async_copy(src, dst, o_s.at[i])
+
     upper(0)
     pl.semaphore_wait(barrier, 12)
+    a_send(0)
     b_spread(0)
-    a_send(0)
     upper(1)
     a_send(1)
     upper(2)
@@ -254,14 +305,16 @@
     upper(3)
     b_home(0)
     b_spread(1)
+    upper(7)
+    send_upper(1)
     upper(4)
-    upper(5)
     a_forward(0)
     a_send(3)
     b_step(0, 1, 0)
     b_step(0, 1, 1)
+    upper(5)
     upper(6)
-    upper(7)
+    send_upper(0)
     a_forward(1)
     a_send(4)
     b_step(0, 2, 0)
@@ -304,32 +357,51 @@
     a_forward(6)
     product(2, 1, Po)
     finish_one(2)
+    product(3, 1, Po)
+    finish_one(3)
+    one_pair()
+    write(0, c1, o1).start()
     a_ready(6)
     c_send(6)
-    product(3, 1, Po)
-    finish_one(3)
-    scatter(P1, R1, r1_s, r1_r)
-    a_forward(7)
     product(4, 1, Po)
     finish_two(0)
+    a_forward(7)
     product(5, 1, Po)
     finish_two(1)
-    gather(P1, R1, G1, r1_r, g1_s, g1_r)
+    scatter(P2, R2, r2_s, r2_r)
+    one_ring()
+    product(6, 1, Po)
+    last_two(0)
     a_ready(7)
     c_send(7)
-    product(6, 1, Po)
     product(7, 1, Po)
-    finish_two(2)
+    last_two(1)
+    scatter(P3, R3, r3_s, r3_r)
+    one_all()
+    gather(P2, R2, G2, r2_r, g2_s, g2_r)
+    gather(P3, R3, G3, r3_r, g3_s, g3_r)
+    cross_two(2)
+    cross_two(3)
+    write(1, c2, o2).start()
     tiles_one()
-    finish_two(3)
-    scatter(P2, R2, r2_s, r2_r)
-    gather(P2, R2, G2, r2_r, g2_s, g2_r)
+    write(2, d1, od1).start()
+    write(3, l2, ol2).start()
     gathered(G2, g2_r)
-    for s in range(SUPERS):
+    gathered(G3, g3_r)
+    for s in range(2):
         d2[s] = d2[s] + G2[:, s].reshape(TILE, TILE)
+        d2[2 + s] = d2[2 + s] + G3[:, s].reshape(TILE, TILE)
+    write(4, d2, od2).start()
     b_spread_done()
     for copy in sends:
         copy.wait_send()
+    for i, (src, dst) in enumerate(((c1, o1), (c2, o2), (d1, od1), (l2, ol2), (d2, od2))):
+        write(i, src, dst).wait()
+
+
+def finish(*refs):
+    for src, dst in zip(refs[:5], refs[5:]):
+        dst[...] = src[...]
 
 
 def local(
@@ -339,12 +411,20 @@
     wide = jax.ShapeDtypeStruct((SUPERS * TILE, WIDE), F32)
     tiles = jax.ShapeDtypeStruct((SUPERS, TILE, TILE), F32)
     dma = pltpu.SemaphoreType.DMA
-    return pl.pallas_call(
+    anywhere = pl.BlockSpec(memory_space=pl.ANY)
+    made = pl.pallas_call(
         kernel,
         out_shape=(wide, tiles, wide, tiles, tiles),
-        in_specs=[vmem] * 8,
-        out_specs=(vmem,) * 5,
+        in_specs=[anywhere, anywhere, vmem, vmem, anywhere, vmem, vmem, vmem],
+        out_specs=(anywhere,) * 5,
         scratch_shapes=[
+            pltpu.VMEM((SUPERS * TILE, WIDE), F32),
+            pltpu.VMEM((SUPERS, TILE, TILE), F32),
+            pltpu.VMEM((SUPERS * TILE, WIDE), F32),
+            pltpu.VMEM((SUPERS, TILE, TILE), F32),
+            pltpu.VMEM((SUPERS, TILE, TILE), F32),
+            pltpu.VMEM((CHUNKS, TILE, WIDE), F32),
+            pltpu.VMEM((2, TILE, WIDE), F32),
             pltpu.VMEM((2, SUPERS, WIDE), F32),
             pltpu.VMEM((4, CHUNKS * TILE, WIDE), F32),
             pltpu.VMEM((CHUNKS, 2 * TILE, 4 * WIDE), BF16),
@@ -354,20 +434,26 @@
             pltpu.VMEM((CHUNKS, TILE, WIDE), F32),
             pltpu.VMEM((CHUNKS, TILE, WIDE), F32),
             pltpu.VMEM((CHUNKS, TILE, WIDE), F32),
-            pltpu.VMEM((8, 2 * SUPERS, 16, TILE), F32),
-            pltpu.VMEM((7, 2 * SUPERS, 16, TILE), F32),
-            pltpu.VMEM((8, 2 * SUPERS, 16, TILE), F32),
-            pltpu.VMEM((8, SUPERS, 16, TILE), F32),
-            pltpu.VMEM((7, SUPERS, 16, TILE), F32),
-            pltpu.VMEM((8, SUPERS, 16, TILE), F32),
+            pltpu.VMEM((2, SUPERS, TILE, TILE), F32),
+            pltpu.VMEM((SUPERS, TILE, TILE), F32),
+            pltpu.VMEM((3, TILE, TILE), F32),
+            pltpu.VMEM((2, SUPERS, TILE, TILE), F32),
+            pltpu.VMEM((8, 2, 16, TILE), F32),
+            pltpu.VMEM((7, 2, 16, TILE), F32),
+            pltpu.VMEM((8, 2, 16, TILE), F32),
+            pltpu.VMEM((8, 2, 16, TILE), F32),
+            pltpu.VMEM((7, 2, 16, TILE), F32),
+            pltpu.VMEM((8, 2, 16, TILE), F32),
             pltpu.VMEM((SUPERS, TILE, TILE), F32),
             dma((2, CHUNKS)), dma((2, CHUNKS)), dma((2, CHUNKS)), dma((2, CHUNKS)),
             dma((2, 2)), dma((2, 2)),
             dma((2, 2, 4, 2)), dma((2, 2, 4, 2)),
             dma((2, 2, 5, 2)), dma((2, 2, 5, 2)),
             dma((CHUNKS,)), dma((CHUNKS,)),
+            dma, dma, dma((3,)), dma((3,)), dma((7,)), dma((7,)),
             dma((7,)), dma((7,)), dma((7,)), dma((7,)),
             dma((7,)), dma((7,)), dma((7,)), dma((7,)),
+            dma((CHUNKS,)), dma((2,)), dma((2,)), dma((5,)),
         ],
         compiler_params=pltpu.CompilerParams(
             collective_id=0, has_side_effects=True, vmem_limit_bytes=60 * 2**20
@@ -376,6 +462,13 @@
             flops=13_000_000_000, bytes_accessed=8_000_000, transcendentals=0
         ),
     )(sigma_sep, factor_one, inverse_one, list_one, factor_two, factor_link, inverse_two, list_two)
+    return pl.pallas_call(
+        finish,
+        out_shape=(wide, tiles, wide, tiles, tiles),
+        in_specs=[vmem] * 5,
+        out_specs=(vmem,) * 5,
+        compiler_params=pltpu.CompilerParams(vmem_limit_bytes=60 * 2**20),
+    )(*made)
 
 
 def solution(mesh):

time: 127 us -> 116 us (0.913)
  local copies, waits for them, and re-layouts: 5.91 us -> 0 us
  Pallas kernels: 120 us -> 115 us
    pallas_call x1, Pallas kernels: 120 us -> 112 us  [local(): pl.pallas_call(kernel, out_shape=(wide, tiles, wide, tiles, tiles), in_sp...]
    unnamed x13 -> x0, local copies, waits for them, and re-layouts: 5.91 us -> none
    pallas_call x0 -> x1, Pallas kernels: none -> 3.33 us  [local(): pl.pallas_call(finish, out_shape=(wide, tiles, wide, tiles, tiles), in_sp...]
where the time goes in v2:
time: 116 us
  Pallas kernels  115 us (99%)
    pallas_call x1, Pallas kernels, local(): pl.pallas_call(kernel, out_shape=(wide, tiles, wide, tiles, tiles), in_sp...  112 us
    pallas_call x1, Pallas kernels, local(): pl.pallas_call(finish, out_shape=(wide, tiles, wide, tiles, tiles), in_sp...  3.33 us

profile of v2, /device:TPU:4, one launch (start us, length us, event | category | flops | bytes accessed | tf_op | source)
XLA Modules:
  0.0 116.0 jit_solution(14503638227855012896)
XLA Ops:
  0.6 112.1 %shard_map.119 = (f32[512,512]{1,0:T(8,128)}, f32[4,128,128]{2,1,0:T(8,128)}, f32[512,512]{1,0:T(8,128)}, f32[4,128,128]{2,1,0:T(8,128)}, f32[4,128,128]{2,1,0:T(8,128)}) custom-call(f32[128,512]{1,0:T(8,128)} %sig.1, f32[512,512]{1,0:T(8,128)} %f1.1, f32[4,128,128]{2,1,0:T(8,128)} %i1.1, s32[4,24]{1,0:T(4,128)} %n1.1, f32[512,512]{1,0:T(8,128)} %f2.1, ...), custom_call_target="tpu_custom_call" | custom-call | flops 12999999488 | bytes 8000000 | tf_op jit(solution)/shard_map/pallas_call | solution.py:415
  112.7 3.3 %shard_map.120 = (f32[512,512]{1,0:T(8,128)}, f32[4,128,128]{2,1,0:T(8,128)}, f32[512,512]{1,0:T(8,128)}, f32[4,128,128]{2,1,0:T(8,128)}, f32[4,128,128]{2,1,0:T(8,128)}) custom-call(f32[512,512]{1,0:T(8,128)} %get-tuple-element.10.refs_0_, f32[4,128,128]{2,1,0:T(8,128)} %get-tuple-element.11.refs_1_, f32[512,512]{1,0:T(8,128)} %get-tuple-element.12.refs_2_, ...), custom_call_target="tpu_custom_call" | custom-call | tf_op jit(solution)/shard_map/pallas_call | solution.py:465

commit v3 on v2

--- a/solution.py
+++ b/solution.py
@@ -32,8 +32,8 @@
 def kernel(
     sig, f1, i1, n1, f2, fl, i2, n2,
     o1, od1, o2, ol2, od2,
-    c1, d1, c2, l2, d2, F, Up, H, A, As, B, Bh, Bl, Cs, Cr, Po, P1, X1, Y1, G1, P2, R2, G2, P3, R3, G3, LU,
-    as_s, as_r, af_s, af_r, bx_s, bx_r, bz_s, bz_r, bc_s, bc_r, c_s, c_r, x1_s, x1_r, y1_s, y1_r, g1_s, g1_r, r2_s, r2_r, g2_s, g2_r,
+    c1, d1, c2, l2, d2, F, Up, H, A, As, B, Bh, Bl, Cs, Cr, Po, P1, R1, G1, P2, R2, G2, P3, R3, G3, LU,
+    as_s, as_r, af_s, af_r, bx_s, bx_r, bz_s, bz_r, bc_s, bc_r, c_s, c_r, r1_s, r1_r, g1_s, g1_r, r2_s, r2_r, g2_s, g2_r,
     r3_s, r3_r, g3_s, g3_r, f_r, u_s, u_r, o_s,
 ):
     row = lax.axis_index("row")
@@ -111,37 +111,39 @@
             As[q, 0:TILE, k * WIDE:(k + 1) * WIDE] = high
             As[q, TILE:2 * TILE, k * WIDE:(k + 1) * WIDE] = low
 
+    pieces = (4, 2)
+
     def b_rows(k, zs, core, h):
-        first = pl.multiple_of(((zs + 8) % 8 * 2 + core) * TILE + h * 64, 64)
-        return B.at[(1 - xl, xl)[k], pl.ds(first, 64), :]
+        size = TILE // pieces[k]
+        first = pl.multiple_of(((zs + 8) % 8 * 2 + core) * TILE + h * size, size)
+        return B.at[(1 - xl, xl)[k], pl.ds(first, size), :]
+
+    def b_out(k, i, h, colt):
+        size = TILE // pieces[k]
+        first = pl.multiple_of((z * 2 + c) * TILE + h * size, size)
+        src, dst = sig.at[pl.ds(h * size, size), :], B.at[xl, pl.ds(first, size), :]
+        return remote(src, dst, bx_s.at[i, h], bx_r.at[k, h], (xh * 4 + y, colt))
 
     def b_spread(k):
-        for h in range(2):
-            src = sig.at[pl.ds(h * 64, 64), :]
-            dst = B.at[xl, pl.ds(pl.multiple_of((z * 2 + c) * TILE + h * 64, 64), 64), :]
-
-            def out(i, colt):
-                return remote(src, dst, bx_s.at[i, h], bx_r.at[k, h], (xh * 4 + y, colt))
-
-            if k == 0:
-                @pl.when(xl != xh)
-                def _():
-                    out(0, z * 2 + c).start()
-                    out(1, 16 + z * 2 + c).start()
-            else:
-                @pl.when(xl == xh)
-                def _():
-                    pltpu.make_async_copy(src, dst, bx_r.at[k, h]).start()
-                    out(0, other_col).start()
+        @pl.when((xl != xh) if k == 0 else (xl == xh))
+        def _():
+            for h in range(pieces[k]):
+                if k == 0:
+                    b_out(k, 0, h, z * 2 + c).start()
+                    b_out(k, 1, h, 16 + z * 2 + c).start()
+                else:
+                    size = TILE // pieces[k]
+                    src = sig.at[pl.ds(h * size, size), :]
+                    pltpu.make_async_copy(src, b_rows(k, z, c, h), bx_r.at[k, h]).start()
+                    b_out(k, 0, h, other_col).start()
 
     def b_spread_done():
-        for h in range(2):
-            src = sig.at[pl.ds(h * 64, 64), :]
-            remote(src, src, bx_s.at[0, h], bx_r.at[0, h], pair).wait_send()
-
-            @pl.when(xl != xh)
+        for k in range(2):
+            @pl.when((xl != xh) if k == 0 else (xl == xh))
             def _():
-                remote(src, src, bx_s.at[1, h], bx_r.at[0, h], pair).wait_send()
+                for h in range(pieces[k]):
+                    for i in range(2 - k):
+                        b_out(k, i, h, other_col).wait_send()
 
     def b_pass(k, d, s, h):
         ref = b_rows(k, z + (-s, s)[d], c, h)
@@ -152,7 +154,7 @@
         start(ref, ref, bc_s.at[k, d, s, h], bc_r.at[k, d, s, h], twin)
 
     def b_home(k):
-        for h in range(2):
+        for h in range(pieces[k]):
             arrived(b_rows(k, z, c, h), bx_r.at[k, h])
             b_pass(k, 0, 0, h)
             b_pass(k, 1, 0, h)
@@ -161,20 +163,21 @@
     def b_step(k, s, h):
         for d in range(2):
             arrived(b_rows(k, z + (-s, s)[d], c, h), bz_r.at[k, d, s - 1, h])
-            if s < 3 or h == d:
+            if s < 3 or h * 2 // pieces[k] == d:
                 b_pass(k, d, s, h)
             b_twin(k, d, s, h)
 
     def b_last(k):
-        for d in range(2):
-            arrived(b_rows(k, z + 4, c, d), bz_r.at[k, d, 3, d])
-            b_twin(k, d, 4, d)
-        for h in range(2):
+        for h in range(pieces[k]):
+            d = h * 2 // pieces[k]
+            arrived(b_rows(k, z + 4, c, h), bz_r.at[k, d, 3, h])
+            b_twin(k, d, 4, h)
+        for h in range(pieces[k]):
             arrived(b_rows(k, z, 1 - c, h), bc_r.at[k, 0, 0, h])
             for d in range(2):
                 for s in range(1, 4):
                     arrived(b_rows(k, z + (-s, s)[d], 1 - c, h), bc_r.at[k, d, s, h])
-            arrived(b_rows(k, z + 4, 1 - c, h), bc_r.at[k, h, 4, h])
+            arrived(b_rows(k, z + 4, 1 - c, h), bc_r.at[k, h * 2 // pieces[k], 4, h])
         which = (1 - xl, xl)[k]
 
         def cut(i, carry):
@@ -199,6 +202,9 @@
 
     def c_send(q):
         product(q, 0, Cs)
+        c_start(q)
+
+    def c_start(q):
         start(Cs.at[q], Cr.at[q], c_s.at[q], c_r.at[q], pair)
 
     def own_upper(q):
@@ -209,8 +215,8 @@
         prod = Po[s] + Cr[s]
         cross = -(hits(0, s) * prod)
         c1[s * TILE:(s + 1) * TILE, :] = cross
-        P1[0, s] = dot3(own_upper(s), prod, 1, 1)
-        P1[1, s] = dot3(cross, own_upper(SUPERS + s), 1, 1)
+        P1[s, 0] = dot3(own_upper(s), prod, 1, 1)
+        P1[s, 1] = dot3(cross, own_upper(SUPERS + s), 1, 1)
 
     def linked(s):
         q = SUPERS + s
@@ -225,7 +231,9 @@
 
     def finish_two(s):
         linked(s)
-        P2[:, s] = dot3(own_upper(SUPERS + s), cross_two(s), 1, 1).reshape(8, 16, TILE)
+        part = dot3(own_upper(SUPERS + s), cross_two(s), 1, 1)
+        P2[2 * s] = part[0:64]
+        P2[2 * s + 1] = part[64:TILE]
 
     def send_upper(i):
         start(A.at[y, pl.ds((6 + i) * TILE, TILE), :], Up.at[i], u_s.at[i], u_r.at[i], pair)
@@ -236,25 +244,28 @@
         part = dot3(own_upper(6 + i), Po[6 + i], 1, 1) + dot3(Up[i], Cs[6 + i], 1, 1)
         P3[:, i] = part.reshape(8, 16, TILE)
 
-    def one_pair():
-        start(P1.at[1 - xl], X1, x1_s, x1_r, pair)
-
-    def one_ring():
-        arrived(X1, x1_r)
-        for s in range(SUPERS):
-            X1[s] = X1[s] + P1[xl, s]
+    def ring_sum(part, got, ss, rs):
         for i in range(3):
             to = (y + i + 1) % 4
-            start(X1.at[to], Y1.at[i], y1_s.at[i], y1_r.at[i], (xl * 4 + to, col))
-
-    def one_all():
-        total = X1[y]
+            start(part.at[to], got.at[i], ss.at[i], rs.at[i], (xl * 4 + to, col))
+
+    def pair_sum(part, got, ss, rs):
+        total = part[y]
         for i in range(3):
-            arrived(Y1.at[i], y1_r.at[i])
-            total = total + Y1[i]
-        G1[xl, y] = total
-        for i, dev in enumerate(peers):
-            start(G1.at[xl, y], G1.at[xl, y], g1_s.at[i], g1_r.at[i], dev)
+            arrived(got.at[i], rs.at[i])
+            total = total + got[i]
+        got[3] = total
+        start(got.at[3], got.at[4], ss.at[3], rs.at[3], pair)
+
+    def ring_all(got, whole, rs, ss, ws):
+        arrived(got.at[4], rs.at[3])
+        whole[y] = got[3] + got[4]
+        for i in range(3):
+            start(whole.at[y], whole.at[y], ss.at[i], ws.at[i], (xl * 4 + (y + i + 1) % 4, col))
+
+    def ring_here(whole, ws):
+        for i in range(3):
+            arrived(whole.at[(y + 3 - i) % 4], ws.at[i])
 
     def scatter(part, got, ss, rs):
         for i, dev in enumerate(peers):
@@ -281,13 +292,11 @@
             d2[s] = dot3(t2, t2, 1, 1)
 
     def tiles_one():
-        for i in range(7):
-            sender = (row + 7 - i) % 8
-            arrived(G1.at[sender // 4, sender % 4], g1_r.at[i])
+        ring_here(G1, g1_r)
         for s in range(SUPERS):
-            diag = d1[s] + G1[0, s]
+            diag = d1[s] + G1[s, 0]
             d1[s] = diag
-            link = G1[1, s] + dot3(diag, LU[s], 1, 1)
+            link = G1[s, 1] + dot3(diag, LU[s], 1, 1)
             l2[s] = -link
             d2[s] = d2[s] + dot3(LU[s], link, 1, 0)
 
@@ -310,20 +319,22 @@
     upper(4)
     a_forward(0)
     a_send(3)
-    b_step(0, 1, 0)
-    b_step(0, 1, 1)
+    for h in range(4):
+        b_step(0, 1, h)
     upper(5)
     upper(6)
     send_upper(0)
     a_forward(1)
     a_send(4)
-    b_step(0, 2, 0)
-    b_step(0, 2, 1)
+    for h in range(4):
+        b_step(0, 2, h)
     side()
     b_step(0, 3, 0)
+    b_step(0, 3, 1)
     a_forward(2)
     a_send(5)
-    b_step(0, 3, 1)
+    b_step(0, 3, 2)
+    b_step(0, 3, 3)
     b_home(1)
     b_last(0)
     a_ready(0)
@@ -359,37 +370,40 @@
     finish_one(2)
     product(3, 1, Po)
     finish_one(3)
-    one_pair()
+    ring_sum(P1, R1, r1_s, r1_r)
     write(0, c1, o1).start()
     a_ready(6)
     c_send(6)
     product(4, 1, Po)
     finish_two(0)
+    pair_sum(P1, R1, r1_s, r1_r)
     a_forward(7)
     product(5, 1, Po)
     finish_two(1)
-    scatter(P2, R2, r2_s, r2_r)
-    one_ring()
+    ring_sum(P2, R2, r2_s, r2_r)
     product(6, 1, Po)
     last_two(0)
     a_ready(7)
-    c_send(7)
+    product(7, 0, Cs)
     product(7, 1, Po)
     last_two(1)
     scatter(P3, R3, r3_s, r3_r)
-    one_all()
-    gather(P2, R2, G2, r2_r, g2_s, g2_r)
+    ring_all(R1, G1, r1_r, g1_s, g1_r)
+    c_start(7)
+    pair_sum(P2, R2, r2_s, r2_r)
     gather(P3, R3, G3, r3_r, g3_s, g3_r)
+    ring_all(R2, G2, r2_r, g2_s, g2_r)
     cross_two(2)
     cross_two(3)
     write(1, c2, o2).start()
     tiles_one()
     write(2, d1, od1).start()
     write(3, l2, ol2).start()
-    gathered(G2, g2_r)
+    ring_here(G2, g2_r)
     gathered(G3, g3_r)
     for s in range(2):
-        d2[s] = d2[s] + G2[:, s].reshape(TILE, TILE)
+        d2[s, 0:64] = d2[s, 0:64] + G2[2 * s]
+        d2[s, 64:TILE] = d2[s, 64:TILE] + G2[2 * s + 1]
         d2[2 + s] = d2[2 + s] + G3[:, s].reshape(TILE, TILE)
     write(4, d2, od2).start()
     b_spread_done()
@@ -434,24 +448,23 @@
             pltpu.VMEM((CHUNKS, TILE, WIDE), F32),
             pltpu.VMEM((CHUNKS, TILE, WIDE), F32),
             pltpu.VMEM((CHUNKS, TILE, WIDE), F32),
-            pltpu.VMEM((2, SUPERS, TILE, TILE), F32),
-            pltpu.VMEM((SUPERS, TILE, TILE), F32),
-            pltpu.VMEM((3, TILE, TILE), F32),
-            pltpu.VMEM((2, SUPERS, TILE, TILE), F32),
-            pltpu.VMEM((8, 2, 16, TILE), F32),
-            pltpu.VMEM((7, 2, 16, TILE), F32),
-            pltpu.VMEM((8, 2, 16, TILE), F32),
+            pltpu.VMEM((SUPERS, 2, TILE, TILE), F32),
+            pltpu.VMEM((5, 2, TILE, TILE), F32),
+            pltpu.VMEM((SUPERS, 2, TILE, TILE), F32),
+            pltpu.VMEM((4, 64, TILE), F32),
+            pltpu.VMEM((5, 64, TILE), F32),
+            pltpu.VMEM((4, 64, TILE), F32),
             pltpu.VMEM((8, 2, 16, TILE), F32),
             pltpu.VMEM((7, 2, 16, TILE), F32),
             pltpu.VMEM((8, 2, 16, TILE), F32),
             pltpu.VMEM((SUPERS, TILE, TILE), F32),
             dma((2, CHUNKS)), dma((2, CHUNKS)), dma((2, CHUNKS)), dma((2, CHUNKS)),
-            dma((2, 2)), dma((2, 2)),
-            dma((2, 2, 4, 2)), dma((2, 2, 4, 2)),
-            dma((2, 2, 5, 2)), dma((2, 2, 5, 2)),
+            dma((2, 4)), dma((2, 4)),
+            dma((2, 2, 4, 4)), dma((2, 2, 4, 4)),
+            dma((2, 2, 5, 4)), dma((2, 2, 5, 4)),
             dma((CHUNKS,)), dma((CHUNKS,)),
-            dma, dma, dma((3,)), dma((3,)), dma((7,)), dma((7,)),
-            dma((7,)), dma((7,)), dma((7,)), dma((7,)),
+            dma((4,)), dma((4,)), dma((3,)), dma((3,)),
+            dma((4,)), dma((4,)), dma((3,)), dma((3,)),
             dma((7,)), dma((7,)), dma((7,)), dma((7,)),
             dma((CHUNKS,)), dma((2,)), dma((2,)), dma((5,)),
         ],

time: 116 us -> 115 us (level)
  no operation moved by 1% of the time
where the time goes in v3:
time: 115 us
  Pallas kernels  114 us (99%)
    pallas_call x1, Pallas kernels, local(): pl.pallas_call(kernel, out_shape=(wide, tiles, wide, tiles, tiles), in_sp...  111 us
    pallas_call x1, Pallas kernels, local(): pl.pallas_call(finish, out_shape=(wide, tiles, wide, tiles, tiles), in_sp...  3.33 us

profile of v3, /device:TPU:4, one launch (start us, length us, event | category | flops | bytes accessed | tf_op | source)
XLA Modules:
  0.0 115.0 jit_solution(8209487586270308274)
XLA Ops:
  0.6 111.0 %shard_map.119 = (f32[512,512]{1,0:T(8,128)}, f32[4,128,128]{2,1,0:T(8,128)}, f32[512,512]{1,0:T(8,128)}, f32[4,128,128]{2,1,0:T(8,128)}, f32[4,128,128]{2,1,0:T(8,128)}) custom-call(f32[128,512]{1,0:T(8,128)} %sig.1, f32[512,512]{1,0:T(8,128)} %f1.1, f32[4,128,128]{2,1,0:T(8,128)} %i1.1, s32[4,24]{1,0:T(4,128)} %n1.1, f32[512,512]{1,0:T(8,128)} %f2.1, ...), custom_call_target="tpu_custom_call" | custom-call | flops 12999999488 | bytes 8000000 | tf_op jit(solution)/shard_map/pallas_call | solution.py:429
  111.6 3.3 %shard_map.120 = (f32[512,512]{1,0:T(8,128)}, f32[4,128,128]{2,1,0:T(8,128)}, f32[512,512]{1,0:T(8,128)}, f32[4,128,128]{2,1,0:T(8,128)}, f32[4,128,128]{2,1,0:T(8,128)}) custom-call(f32[512,512]{1,0:T(8,128)} %get-tuple-element.10.refs_0_, f32[4,128,128]{2,1,0:T(8,128)} %get-tuple-element.11.refs_1_, f32[512,512]{1,0:T(8,128)} %get-tuple-element.12.refs_2_, ...), custom_call_target="tpu_custom_call" | custom-call | tf_op jit(solution)/shard_map/pallas_call | solution.py:478

commit v4 on v3

--- a/solution.py
+++ b/solution.py
@@ -359,30 +359,26 @@
     c_send(4)
     a_forward(5)
     b_last(1)
-    product(0, 1, Po)
     a_ready(5)
     c_send(5)
-    finish_one(0)
-    product(1, 1, Po)
-    finish_one(1)
     a_forward(6)
-    product(2, 1, Po)
-    finish_one(2)
-    product(3, 1, Po)
-    finish_one(3)
+    for s in range(4):
+        product(s, 1, Po)
+        finish_one(s)
+        if s == 2:
+            a_forward(7)
     ring_sum(P1, R1, r1_s, r1_r)
-    write(0, c1, o1).start()
     a_ready(6)
     c_send(6)
+    write(0, c1, o1).start()
     product(4, 1, Po)
     finish_two(0)
-    pair_sum(P1, R1, r1_s, r1_r)
-    a_forward(7)
     product(5, 1, Po)
     finish_two(1)
     ring_sum(P2, R2, r2_s, r2_r)
     product(6, 1, Po)
     last_two(0)
+    pair_sum(P1, R1, r1_s, r1_r)
     a_ready(7)
     product(7, 0, Cs)
     product(7, 1, Po)

time: 115 us -> 113 us (0.983)
  Pallas kernels: 114 us -> 112 us
    pallas_call x1, Pallas kernels: 111 us -> 109 us  [local(): pl.pallas_call(kernel, out_shape=(wide, tiles, wide, tiles, tiles), in_sp...]
where the time goes in v4:
time: 113 us
  Pallas kernels  112 us (99%)
    pallas_call x1, Pallas kernels, local(): pl.pallas_call(kernel, out_shape=(wide, tiles, wide, tiles, tiles), in_sp...  109 us
    pallas_call x1, Pallas kernels, local(): pl.pallas_call(finish, out_shape=(wide, tiles, wide, tiles, tiles), in_sp...  3.33 us

profile of v4, /device:TPU:4, one launch (start us, length us, event | category | flops | bytes accessed | tf_op | source)
XLA Modules:
  0.0 112.9 jit_solution(4772390806071047986)
XLA Ops:
  0.6 108.9 %shard_map.119 = (f32[512,512]{1,0:T(8,128)}, f32[4,128,128]{2,1,0:T(8,128)}, f32[512,512]{1,0:T(8,128)}, f32[4,128,128]{2,1,0:T(8,128)}, f32[4,128,128]{2,1,0:T(8,128)}) custom-call(f32[128,512]{1,0:T(8,128)} %sig.1, f32[512,512]{1,0:T(8,128)} %f1.1, f32[4,128,128]{2,1,0:T(8,128)} %i1.1, s32[4,24]{1,0:T(4,128)} %n1.1, f32[512,512]{1,0:T(8,128)} %f2.1, ...), custom_call_target="tpu_custom_call" | custom-call | flops 12999999488 | bytes 8000000 | tf_op jit(solution)/shard_map/pallas_call | solution.py:425
  109.6 3.3 %shard_map.120 = (f32[512,512]{1,0:T(8,128)}, f32[4,128,128]{2,1,0:T(8,128)}, f32[512,512]{1,0:T(8,128)}, f32[4,128,128]{2,1,0:T(8,128)}, f32[4,128,128]{2,1,0:T(8,128)}) custom-call(f32[512,512]{1,0:T(8,128)} %get-tuple-element.10.refs_0_, f32[4,128,128]{2,1,0:T(8,128)} %get-tuple-element.11.refs_1_, f32[512,512]{1,0:T(8,128)} %get-tuple-element.12.refs_2_, ...), custom_call_target="tpu_custom_call" | custom-call | tf_op jit(solution)/shard_map/pallas_call | solution.py:474
